TPU v7x, 256 devices: a whole 4x4x8 slice. The times are simulated.
256 devices in a mesh: dp: 32 (over z, x), fsdp: 2 (over core), tensor: 4 (over y).
Axes of the slice: x: 4, y: 4, z: 8, core: 2. Of those that a mesh axis runs over, the one named last changes fastest.
Arguments:
- activations: bfloat16 [1, 16384, 8192], P(None, ('dp', 'tensor'), 'fsdp'), may hold values from -6 to 6
- cotangents: bfloat16 [1, 16384, 28672], P(None, ('dp', 'fsdp'), 'tensor'), may hold values from -16 to 16
- projector: bfloat16 [8192, 1024], P('fsdp'), may hold values from -0.0625 to 0.0625
- first_moment: float32 [1, 4, 7168, 1024], P(None, 'tensor', 'dp', 'fsdp'), may hold values from -60 to 60
- second_moment: float32 [1, 4, 7168, 1024], P(None, 'tensor', 'dp', 'fsdp'), may hold values from 1 to 16
Outputs:
- update: float32 [1, 4, 7168, 8192], P(None, 'tensor', 'dp', 'fsdp')
- new_first: float32 [1, 4, 7168, 1024], P(None, 'tensor', 'dp', 'fsdp')
- new_second: float32 [1, 4, 7168, 1024], P(None, 'tensor', 'dp', 'fsdp')
All inputs are finite; a program needn't handle non-finite values.
Results may differ from a plain program's by a relative error of at most 0.029.
Values may be sent and summed in bfloat16 or wider, within the bound.
A program may use at most 128 MiB of HBM per device.

v0:
```python
import jax
import jax.numpy as jnp
from jax import lax
from jax.sharding import PartitionSpec as P

beta_first = 0.9
beta_second = 0.999
bias_first = 1.0 - 0.9**10
bias_second = 1.0 - 0.999**10
adam_eps = 1e-08


def per_device(activations, cotangents, projector, first_moment, second_moment):
    fsdp_index = lax.axis_index("fsdp")
    rank_part = projector.shape[1] // lax.axis_size("fsdp")
    partial_proj = jnp.dot(activations[0], projector, preferred_element_type=jnp.float32)
    summed = lax.psum(partial_proj, "fsdp")
    own_share = lax.dynamic_slice_in_dim(summed, fsdp_index * rank_part, rank_part, 1)
    own_share = own_share.astype(jnp.bfloat16)
    projected = lax.all_gather(own_share, "tensor", axis=0, tiled=True)
    gathered = lax.all_gather(cotangents[0], "fsdp", axis=0, tiled=True)
    lowrank = lax.psum_scatter(
        lax.dot_general(
            gathered, projected, (((0,), (0,)), ((), ())), preferred_element_type=jnp.float32
        ).astype(jnp.bfloat16),
        "dp",
        scatter_dimension=0,
        tiled=True,
    ).astype(jnp.float32)
    moment = first_moment[0, 0]
    second = second_moment[0, 0]
    fresh_first = beta_first * moment + (1.0 - beta_first) * lowrank
    fresh_second = beta_second * second + (1.0 - beta_second) * lowrank * lowrank
    direction = (
        fresh_first / bias_first / (jnp.sqrt(fresh_second / bias_second) + adam_eps)
    ).astype(jnp.bfloat16)
    update = lax.dot_general(
        lax.all_gather(direction, "fsdp", axis=1, tiled=True),
        projector,
        (((1,), (1,)), ((), ())),
        preferred_element_type=jnp.float32,
    )
    updates = [update[None]]
    firsts = [fresh_first[None]]
    seconds = [fresh_second[None]]
    return (jnp.stack(updates), jnp.stack(firsts), jnp.stack(seconds))


def solution(mesh):
    return jax.shard_map(
        per_device,
        mesh=mesh,
        in_specs=(
            P(None, ("dp", "tensor"), "fsdp"),
            P(None, ("dp", "fsdp"), "tensor"),
            P("fsdp", None),
            P(None, "tensor", "dp", "fsdp"),
            P(None, "tensor", "dp", "fsdp"),
        ),
        out_specs=(
            P(None, "tensor", "dp", "fsdp"),
            P(None, "tensor", "dp", "fsdp"),
            P(None, "tensor", "dp", "fsdp"),
        ),
        check_vma=False,
    )
```

profile of v0, /device:TPU:1, one launch (start us, length us, event | category | flops | bytes accessed | tf_op | source)
XLA Modules:
  0.0 306.9 jit_solution(6491711950355695806)
XLA Ops:
  7.2 0.0 copy-start
  7.2 0.0 all-gather.3.cloned.1.call-start
  7.2 0.7 all-gather.3.cloned.1.call-update
  7.9 0.0 reduce-scatter.4.cloned.1.call-start
  8.0 0.4 copy-done
  8.4 4.6 %fusion.2 = f32[128,1024]{1,0:T(8,128)S(1)} fusion(bf16[4096,1024]{1,0:T(8,128)(2,1)} %param.7, bf16[1,128,4096]{2,1,0:T(8,128)(2,1)S(1)} %copy-done), kind=kOutput, calls=%fused_computation.4 | convolution fusion | flops 1073741824 | bytes 9961472 | tf_op jit(solution)/shard_map/dot_general | solution.py:16
  13.0 7.9 %all-reduce.1 = bf16[128,1024]{1,0:T(8,128)(2,1)S(1)} all-reduce(f32[128,1024]{1,0:T(8,128)S(1)} %fusion.2), channel_id=1, replica_groups=mesh['dp'=32,'fsdp'=2,'tensor'=4] {'fsdp'}, use_global_device_ids=true, to_apply=%region_0.0 | all-reduce | flops 131072 | bytes 786432 | tf_op jit(solution)/shard_map/psum | solution.py:17
  21.0 10.3 %all_gather.9 = bf16[512,512]{1,0:T(8,128)(2,1)S(1)} all-gather(bf16[128,512]{1,0:T(8,128)(2,1)S(1)} %dynamic-slice_convert_fusion), channel_id=1, replica_groups=mesh['dp'=32,'fsdp'=2,'tensor'=4] {'tensor'}, dimensions={0}, use_global_device_ids=true | all-gather | bytes 655360 | tf_op jit(solution)/shard_map/all_gather | solution.py:20
  31.3 6.7 %all-gather.3.cloned.1.call-done = bf16[1,512,7168]{2,1,0:T(8,128)(2,1)} async-done(((bf16[1,256,7168]{2,1,0:T(8,128)(2,1)}), bf16[1,512,7168]{2,1,0:T(8,128)(2,1)}) %all-gather.3.cloned.1.call-update) | async-done | bytes 7340048 | tf_op jit(solution)/shard_map/all_gather | solution.py:21
  38.0 9.1 %fusion = bf16[7168,512]{0,1:T(8,128)(2,1)} fusion(bf16[512,512]{1,0:T(8,128)(2,1)S(1)} %all_gather.9, bf16[1,512,7168]{2,1,0:T(8,128)(2,1)} %all-gather.3.cloned.1.call-done), kind=kOutput, calls=%fused_computation.1 | convolution fusion | flops 3761766400 | bytes 15204352 | tf_op jit(solution)/shard_map/dot_general | solution.py:23
  47.2 10.4 %copy.16 = bf16[7168,512]{1,0:T(8,128)(2,1)} copy(bf16[7168,512]{0,1:T(8,128)(2,1)} %fusion) | data formatting | bytes 14680064
  57.6 0.0 copy-start.1
  57.6 0.0 copy-start.2
  57.6 0.0 reduce-scatter.4.cloned.1.call-update
  57.6 1.0 copy-done.1
  58.6 0.2 copy.12
  58.8 0.0 copy-done.2
  58.8 0.2 copy.13
  59.0 221.7 %reduce-scatter.4.cloned.1.call-done = bf16[224,512]{1,0:T(8,128)(2,1)} async-done(((bf16[7168,512]{1,0:T(8,128)(2,1)}), bf16[224,512]{1,0:T(8,128)(2,1)}) %reduce-scatter.4.cloned.1.call-update) | async-done | bytes 229392
  280.7 1.8 copy.17
  282.5 1.3 fusion.7
  283.8 1.0 copy.15
  284.7 1.0 copy.14
  285.7 6.4 %all_gather.11 = bf16[224,1024]{0,1:T(8,128)(2,1)S(1)} all-gather(bf16[224,512]{0,1:T(8,128)(2,1)S(1)} %get-tuple-element.10), channel_id=1, replica_groups=mesh['dp'=32,'fsdp'=2,'tensor'=4] {'fsdp'}, dimensions={1}, use_global_device_ids=true | all-gather | bytes 688128 | tf_op jit(solution)/shard_map/all_gather | solution.py:38
  292.1 7.9 %convolution_bitcast_fusion = f32[1,1,224,4096]{3,2,1,0:T(8,128)} fusion(bf16[224,1024]{0,1:T(8,128)(2,1)S(1)} %all_gather.11, bf16[4096,1024]{1,0:T(8,128)(2,1)} %param.7), kind=kOutput, calls=%fused_computation.3 | convolution fusion | flops 1879048192 | bytes 12517376 | tf_op jit(solution)/shard_map/dot_general | solution.py:37
  (1 shorter events, 0.0 us)
Async XLA Ops:
  7.2 1.2 copy-start
  7.2 30.8 %all-gather.3.cloned.1.call-start = ((), (), s32[]{:S(2)}) async-start(), calls=%async_computation.1 | async-start | bytes 11010048 | tf_op jit(solution)/shard_map/all_gather | solution.py:21
  7.9 272.8 %reduce-scatter.4.cloned.1.call-start = ((), (), s32[]{:S(2)}) async-start(), calls=%async_computation.2 | async-start | bytes 7569408
  57.6 1.0 copy-start.1
  57.6 1.2 copy-start.2
Sparse Core Ops, SparseCore 0:
  9.8 28.1 all-gather.2
  57.7 222.8 reduce-scatter.3
where the time goes:
time: 307 us
  waiting for transfers between devices  229 us (75%)
  blocking collectives  24.7 us (8%)
  matrix products  21.7 us (7%)
  local copies, waits for them, and re-layouts  16 us (5%)
  between operations  14.1 us (5%)
    unnamed x3, waiting for transfers between devices  222 us
    unnamed x12, local copies, waits for them, and re-layouts  15.9 us
    all_gather x1, blocking collectives, per_device(): projected = lax.all_gather(own_share, 'tensor', axis=0, tiled=True)  10.3 us
    dot_general x1, matrix products, per_device(): lax.dot_general(gathered, projected, (((0,), (0,)), ((), ())), preferred_...  9.14 us
    psum x1, blocking collectives, per_device(): summed = lax.psum(partial_proj, 'fsdp')  7.93 us
    dot_general x1, matrix products, per_device(): lax.dot_general(lax.all_gather(direction, 'fsdp', axis=1, tiled=True), pr...  7.91 us
    all_gather x1, waiting for transfers between devices, per_device(): gathered = lax.all_gather(cotangents[0], 'fsdp', axis=0, tiled=True)  6.69 us
    all_gather x1, blocking collectives, per_device(): lax.all_gather(direction, 'fsdp', axis=1, tiled=True)  6.4 us
  transfers between devices with their start and end apart: 2, of which 2 were waited for; matrix products, arithmetic and copies ran while one was open for 2% of the time, Pallas kernels for 0%

commit v1 on v0

v1 whole, which is shorter than its diff:
```python
import functools

import jax
import jax.numpy as jnp
from jax import lax
from jax.experimental import pallas as pl
from jax.experimental.pallas import tpu as pltpu
from jax.sharding import PartitionSpec as P

beta_first = 0.9
beta_second = 0.999
bias_first = 1.0 - 0.9**10
bias_second = 1.0 - 0.999**10
adam_eps = 1e-08

NZ, NX, NY = 8, 4, 4
TOK = 128
WIDTH = 4096
RANK = 1024
HALF = 512
ROWS = 224
UNIT = NX * ROWS
HID = NZ * UNIT
RX = 128
RZ = ROWS - RX
QUARTER = HALF // 2
KCH = 4
F32, BF16 = jnp.float32, jnp.bfloat16
MESH = pl.DeviceIdType.MESH

STEPS = (4, 3, -3, 2, -2, 1, -1, 0)


def dot(a, b, dims):
    return lax.dot_general(a, b, (dims, ((), ())), preferred_element_type=F32)


def kernel(
    act, cot, projector, first, second, upd, new_first, new_second,
    act_v, prj_v, cot_v, part_v, other_v, proj_v, term, xr, zz, zx, xz, dir_v, first_v, second_v,
    load, cot_load, cot_s, cot_r, part_s, part_r, y_s, y_r, xr_s, xr_r, zz_s, zz_r,
    zx_s, zx_r, xz_s, xz_r, dir_s, dir_r,
):
    dp, core, y = lax.axis_index("dp"), lax.axis_index("fsdp"), lax.axis_index("tensor")
    z, x = dp // NX, dp % NX

    def at_x(k):
        return (z * NX + (x + k + NX) % NX, core, y)

    def at_z(k):
        return (((z + k + NZ) % NZ) * NX + x, core, y)

    def at_y(k):
        return (dp, core, (y + k) % NY)

    sibling = (dp, 1 - core, y)

    def remote(src, dst, send, recv, device):
        return pltpu.make_async_remote_copy(
            src_ref=src, dst_ref=dst, send_sem=send, recv_sem=recv, device_id=device, device_id_type=MESH
        )

    def unit_cols(i):
        return pl.ds(pl.multiple_of(((z + STEPS[i] + NZ) % NZ) * UNIT, UNIT), UNIT)

    own_tok = pl.ds(pl.multiple_of(core * 256, 256), 256)
    loads = [pltpu.make_async_copy(act.at[0], act_v, load.at[0])]
    kk = WIDTH // KCH
    for c in range(KCH):
        rows = pl.ds(c * kk, kk)
        loads.append(pltpu.make_async_copy(projector.at[rows], prj_v.at[rows], load.at[1 + c]))
    loads.append(pltpu.make_async_copy(first.at[0, 0], first_v, load.at[1 + KCH]))
    loads.append(pltpu.make_async_copy(second.at[0, 0], second_v, load.at[2 + KCH]))
    for c in loads[: 1 + KCH]:
        c.start()
    cot_in = [
        pltpu.make_async_copy(cot.at[0, :, unit_cols(i)], cot_v.at[own_tok, unit_cols(i)], cot_load.at[i])
        for i in range(NZ)
    ]
    for c in cot_in:
        c.start()
    for c in loads[1 + KCH :]:
        c.start()

    barrier = pltpu.get_barrier_semaphore()
    for device in (sibling, at_y(1), at_y(2), at_y(3), at_x(1), at_x(-1), at_z(1), at_z(-1)):
        pl.semaphore_signal(barrier, inc=1, device_id=device, device_id_type=MESH)
    pl.semaphore_wait(barrier, 8)

    cot_x = [
        remote(cot.at[0, :, unit_cols(i)], cot_v.at[own_tok, unit_cols(i)], cot_s.at[i], cot_r.at[i], sibling)
        for i in range(NZ)
    ]
    for c in cot_x[:2]:
        c.start()

    loads[0].wait()
    for c in range(KCH):
        loads[1 + c].wait()
        piece = dot(act_v[:, c * kk : (c + 1) * kk], prj_v[c * kk : (c + 1) * kk, :], ((1,), (0,)))
        for h in range(2):
            block = piece[:, h * HALF : (h + 1) * HALF]
            if c == 0:
                part_v[h] = block
            else:
                part_v[h] += block
    swap = remote(part_v.at[1 - core], other_v, part_s.at[0], part_r.at[0], sibling)
    swap.start()
    for c in cot_x[2:]:
        c.start()
    swap.wait_recv()
    own_rows = pl.ds(pl.multiple_of(y * TOK, TOK), TOK)
    proj_v[own_rows, :] = (part_v[core] + other_v[...]).astype(BF16)
    gather = [
        remote(proj_v.at[own_rows], proj_v.at[own_rows], y_s.at[k - 1], y_r.at[k - 1], at_y(k)) for k in (2, 1, 3)
    ]
    for c in gather:
        c.start()
    for c in gather:
        c.wait_recv()

    def place(i, j, first_row, rows):
        base = ((z + STEPS[i] + NZ) % NZ) * UNIT + ((x + j + NX) % NX) * ROWS + first_row
        return pl.ds(pl.multiple_of(base, 32), rows)

    def x_rows(i, j):
        return place(i, j, 0, RX)

    def z_rows(i, j):
        return place(i, j, RX, RZ)

    def compute(i):
        cot_in[i].wait()
        cot_x[i].wait_recv()
        term[unit_cols(i), :] = dot(cot_v[:, unit_cols(i)], proj_v[...], ((0,), (0,))).astype(BF16)

    sends = list(cot_x) + [swap] + gather

    def start(copy):
        copy.start()
        sends.append(copy)
        return copy

    x_first = {}

    def x_open(i):
        s = 1 - 2 * (i % 2)
        x_first[i, 0] = start(
            remote(term.at[x_rows(i, 2 * s)], xr.at[i, 0], xr_s.at[i, 0], xr_r.at[i, 0], at_x(s))
        )
        x_first[i, 2] = start(
            remote(term.at[x_rows(i, -s)], xr.at[i, 2], xr_s.at[i, 2], xr_r.at[i, 2], at_x(-s))
        )

    def x_forward(i):
        s = 1 - 2 * (i % 2)
        x_first[i, 0].wait_recv()
        rows = x_rows(i, s)
        term[rows, :] = term[rows, :] + xr[i, 0]
        x_first[i, 1] = start(remote(term.at[rows], xr.at[i, 1], xr_s.at[i, 1], xr_r.at[i, 1], at_x(s)))

    zx_copies = {}

    def x_close(i):
        x_first[i, 1].wait_recv()
        x_first[i, 2].wait_recv()
        rows = x_rows(i, 0)
        total = term[rows, :].astype(F32) + xr[i, 1].astype(F32) + xr[i, 2].astype(F32)
        if i == 0:
            term[rows, :] = total.astype(BF16)
            for n, (s, lanes) in enumerate(((1, pl.ds(0, QUARTER)), (-1, pl.ds(QUARTER, QUARTER)))):
                zx_copies[0, s] = start(
                    remote(term.at[rows, lanes], zx.at[0, :, lanes], zx_s.at[7 * n], zx_r.at[7 * n], at_z(s))
                )
            return None
        if i == 7:
            zx_copies[5].wait_recv()
            zx_copies[6].wait_recv()
            return total + zx[5].astype(F32) + zx[6].astype(F32)
        s = 1 if STEPS[i] > 0 else -1
        if i in (1, 2):
            lanes = slice(0, QUARTER) if s == 1 else slice(QUARTER, HALF)
            rest = slice(QUARTER, HALF) if s == 1 else slice(0, QUARTER)
            zx_copies[0, s].wait_recv()
            term[rows, lanes] = (total[:, lanes] + zx[0, :, lanes].astype(F32)).astype(BF16)
            term[rows, rest] = total[:, rest].astype(BF16)
        else:
            zx_copies[i - 2].wait_recv()
            term[rows, :] = (total + zx[i - 2].astype(F32)).astype(BF16)
        zx_copies[i] = start(remote(term.at[rows], zx.at[i], zx_s.at[i], zx_r.at[i], at_z(s)))
        return None

    zz_copies = {}

    def z_step(i):
        s = 1 if STEPS[i] > 0 else -1
        for j in range(NX):
            rows = z_rows(i, j)
            if i == 0:
                s = 1 if j < 2 else -1
            elif i in (1, 2):
                if (j < 2) == (s == 1):
                    zz_copies[0, j].wait_recv()
                    term[rows, :] = term[rows, :] + zz[0, j]
            elif i < 7:
                zz_copies[i - 2, j].wait_recv()
                term[rows, :] = term[rows, :] + zz[i - 2, j]
            zz_copies[i, j] = start(
                remote(term.at[rows], zz.at[i, j], zz_s.at[i, j], zz_r.at[i, j], at_z(s))
            )

    def z_total(j):
        zz_copies[5, j].wait_recv()
        zz_copies[6, j].wait_recv()
        return term[z_rows(7, j), :].astype(F32) + zz[5, j].astype(F32) + zz[6, j].astype(F32)

    xz_copies = {}

    def z_open():
        rows = z_rows(7, 2)
        term[rows, :] = z_total(2).astype(BF16)
        for n, (s, lanes) in enumerate(((1, pl.ds(0, QUARTER)), (-1, pl.ds(QUARTER, QUARTER)))):
            xz_copies[0, s] = start(
                remote(term.at[rows, lanes], xz.at[0, :, lanes], xz_s.at[3 * n], xz_r.at[3 * n], at_x(s))
            )

    def z_forward(n):
        s = 1 if n == 1 else -1
        j = s % NX
        total = z_total(j)
        lanes = slice(0, QUARTER) if s == 1 else slice(QUARTER, HALF)
        rest = slice(QUARTER, HALF) if s == 1 else slice(0, QUARTER)
        rows = z_rows(7, j)
        xz_copies[0, s].wait_recv()
        term[rows, lanes] = (total[:, lanes] + xz[0, :, lanes].astype(F32)).astype(BF16)
        term[rows, rest] = total[:, rest].astype(BF16)
        xz_copies[n] = start(remote(term.at[rows], xz.at[n], xz_s.at[n], xz_r.at[n], at_x(s)))

    def z_close():
        total = z_total(0)
        xz_copies[1].wait_recv()
        xz_copies[2].wait_recv()
        return total + xz[1].astype(F32) + xz[2].astype(F32)

    dir_copies = []
    own_lanes = pl.ds(pl.multiple_of(core * HALF, HALF), HALF)

    def adam(lowrank, rows):
        fresh_first = beta_first * first_v[rows, :] + (1.0 - beta_first) * lowrank
        fresh_second = beta_second * second_v[rows, :] + (1.0 - beta_second) * lowrank * lowrank
        new_first[0, 0, rows, :] = fresh_first
        new_second[0, 0, rows, :] = fresh_second
        direction = fresh_first / bias_first / (jnp.sqrt(fresh_second / bias_second) + adam_eps)
        dir_v[rows, own_lanes] = direction.astype(BF16)
        n = len(dir_copies)
        dir_copies.append(
            start(
                remote(dir_v.at[rows, own_lanes], dir_v.at[rows, own_lanes], dir_s.at[n], dir_r.at[n], sibling)
            )
        )

    def back_project(n, rows):
        dir_copies[n].wait_recv()
        left = dir_v[rows, :]
        for c in range(8):
            cols = slice(c * 512, (c + 1) * 512)
            upd[0, 0, rows, cols] = dot(left, prj_v[cols, :], ((1,), (1,)))

    compute(0), x_open(0), z_step(0)
    compute(1), x_open(1), z_step(1)
    compute(2), x_open(2), z_step(2)
    compute(3), x_open(3), x_forward(0)
    compute(4), x_open(4), x_forward(1)
    z_step(3), z_step(4), x_close(0)
    compute(5), x_open(5), x_forward(2)
    compute(6), x_open(6), x_close(1)
    compute(7), x_open(7), x_forward(3)
    x_close(2), x_forward(4)
    z_step(5), z_step(6)
    x_close(3), x_forward(5)
    x_close(4), x_forward(6)
    x_close(5), x_forward(7)
    z_open(), x_close(6)
    z_forward(1), z_forward(2)
    for c in loads[1 + KCH :]:
        c.wait()
    z_rows_own, x_rows_own = pl.ds(RX, RZ), pl.ds(0, RX)
    adam(z_close(), z_rows_own)
    back_project(0, z_rows_own)
    adam(x_close(7), x_rows_own)
    back_project(1, x_rows_own)
    for c in sends:
        c.wait_send()


def per_device(activations, cotangents, projector, first_moment, second_moment):
    any_space = pl.BlockSpec(memory_space=pl.ANY)
    vmem = pl.BlockSpec(memory_space=pltpu.VMEM)
    dma = pltpu.SemaphoreType.DMA
    return pl.pallas_call(
        kernel,
        out_shape=(
            jax.ShapeDtypeStruct((1, 1, ROWS, WIDTH), F32),
            jax.ShapeDtypeStruct((1, 1, ROWS, HALF), F32),
            jax.ShapeDtypeStruct((1, 1, ROWS, HALF), F32),
        ),
        in_specs=[any_space] * 5,
        out_specs=(vmem, vmem, vmem),
        scratch_shapes=[
            pltpu.VMEM((TOK, WIDTH), BF16),
            pltpu.VMEM((WIDTH, RANK), BF16),
            pltpu.VMEM((512, HID), BF16),
            pltpu.VMEM((2, TOK, HALF), F32),
            pltpu.VMEM((TOK, HALF), F32),
            pltpu.VMEM((512, HALF), BF16),
            pltpu.VMEM((HID, HALF), BF16),
            pltpu.VMEM((8, 3, RX, HALF), BF16),
            pltpu.VMEM((7, NX, RZ, HALF), BF16),
            pltpu.VMEM((7, RX, HALF), BF16),
            pltpu.VMEM((3, RZ, HALF), BF16),
            pltpu.VMEM((ROWS, RANK), BF16),
            pltpu.VMEM((ROWS, HALF), F32),
            pltpu.VMEM((ROWS, HALF), F32),
            dma((3 + KCH,)),
            dma((8,)),
            dma((8,)),
            dma((8,)),
            dma((1,)),
            dma((1,)),
            dma((3,)),
            dma((3,)),
            dma((8, 3)),
            dma((8, 3)),
            dma((7, NX)),
            dma((7, NX)),
            dma((8,)),
            dma((8,)),
            dma((4,)),
            dma((4,)),
            dma((2,)),
            dma((2,)),
        ],
        compiler_params=pltpu.CompilerParams(
            collective_id=0, has_side_effects=True, vmem_limit_bytes=56 * 2**20
        ),
        name="galore_step",
    )(activations, cotangents, projector, first_moment, second_moment)


def solution(mesh):
    return jax.shard_map(
        per_device,
        mesh=mesh,
        in_specs=(
            P(None, ("dp", "tensor"), "fsdp"),
            P(None, ("dp", "fsdp"), "tensor"),
            P("fsdp", None),
            P(None, "tensor", "dp", "fsdp"),
            P(None, "tensor", "dp", "fsdp"),
        ),
        out_specs=(
            P(None, "tensor", "dp", "fsdp"),
            P(None, "tensor", "dp", "fsdp"),
            P(None, "tensor", "dp", "fsdp"),
        ),
        check_vma=False,
    )
```

time: 307 us -> 90.3 us (0.29)
  waiting for transfers between devices: 229 us -> 0 us
  Pallas kernels: 0 us -> 83.7 us
  blocking collectives: 24.7 us -> 0 us
  matrix products: 21.7 us -> 0 us
  between operations: 14.1 us -> 0.66 us
  local copies, waits for them, and re-layouts: 16 us -> 5.9 us
    unnamed x3 -> x0, waiting for transfers between devices: 222 us -> none
    pallas_call x0 -> x1, Pallas kernels: none -> 83.7 us  [per_device(): pl.pallas_call(kernel, out_shape=(jax.ShapeDtypeStruct((1, 1, ROWS, WIDTH...]
    dot_general x3 -> x0, matrix products: 21.7 us -> none  [the longest x1 9.14 us: per_device(): lax.dot_general(gathered, projected, (((0,), (0,)), ((), ())), preferred_...]
    all_gather x2 -> x0, blocking collectives: 16.7 us -> none  [the longest x1 10.3 us: per_device(): projected = lax.all_gather(own_share, 'tensor', axis=0, tiled=True)]
    unnamed x12 -> x7, local copies, waits for them, and re-layouts: 15.9 us -> 5.9 us
    psum x1 -> x0, blocking collectives: 7.93 us -> none  [per_device(): summed = lax.psum(partial_proj, 'fsdp')]
    all_gather x1 -> x0, waiting for transfers between devices: 6.69 us -> none  [per_device(): gathered = lax.all_gather(cotangents[0], 'fsdp', axis=0, tiled=True)]
  transfers between devices with their start and end apart: 2 -> 0, of which waited for: 2 -> 0; matrix products, arithmetic and copies ran while one was open for 2% -> 0% of each run, Pallas kernels for 0% -> 0%
where the time goes in v1:
time: 90.3 us; the launch traced here: 90.2 us
  Pallas kernels  83.7 us (93%)
  local copies, waits for them, and re-layouts  5.9 us (7%)
    pallas_call x1, Pallas kernels, per_device(): pl.pallas_call(kernel, out_shape=(jax.ShapeDtypeStruct((1, 1, ROWS, WIDTH...  83.7 us
    unnamed x7, local copies, waits for them, and re-layouts  5.9 us

profile of v1, /device:TPU:1, one launch (start us, length us, event | category | flops | bytes accessed | tf_op | source)
XLA Modules:
  0.0 90.2 jit_solution(10275158263513988233)
XLA Ops:
  0.6 83.7 %galore_step.1 = (f32[1,1,224,4096]{3,2,1,0:T(8,128)}, f32[1,1,224,512]{3,2,1,0:T(8,128)}, f32[1,1,224,512]{3,2,1,0:T(8,128)}) custom-call(bf16[1,128,4096]{2,1,0:T(8,128)(2,1)} %act.1, bf16[1,256,7168]{2,1,0:T(8,128)(2,1)} %cot.1, bf16[4096,1024]{1,0:T(8,128)(2,1)} %projector.1, f32[1,1,224,512]{3,2,1,0:T(8,128)} %first.1, f32[1,1,224,512]{3,2,1,0:T(8,128)} %second.1), custom_call_target="tpu_custom_call" | custom-call | tf_op jit(solution)/shard_map/galore_step/pallas_call | solution.py:300
  84.3 0.0 copy-start.1
  84.3 0.0 copy-start
  84.3 4.4 %copy.11 = f32[1,1,224,4096]{3,2,1,0:T(8,128)} copy(f32[1,1,224,4096]{3,2,1,0:T(8,128)} %get-tuple-element.6) | data formatting | bytes 7340032
  88.7 0.0 copy-done.1
  88.7 0.8 copy.12
  89.4 0.0 copy-done
  89.4 0.8 copy.13
Async XLA Ops:
  84.3 4.4 %copy-start.1 = (f32[1,1,224,512]{3,2,1,0:T(8,128)S(1)}, f32[1,1,224,512]{3,2,1,0:T(8,128)}, u32[]{:S(2)}) copy-start(f32[1,1,224,512]{3,2,1,0:T(8,128)} %get-tuple-element.7) | copy-start | bytes 1376260
  84.3 5.1 %copy-start = (f32[1,1,224,512]{3,2,1,0:T(8,128)S(1)}, f32[1,1,224,512]{3,2,1,0:T(8,128)}, u32[]{:S(2)}) copy-start(f32[1,1,224,512]{3,2,1,0:T(8,128)} %get-tuple-element.8) | copy-start | bytes 1376260

commit v2 on v1

--- a/solution.py
+++ b/solution.py
@@ -25,19 +25,28 @@
 RZ = ROWS - RX
 QUARTER = HALF // 2
 KCH = 4
+COLS = 512
 F32, BF16 = jnp.float32, jnp.bfloat16
 MESH = pl.DeviceIdType.MESH
 
 STEPS = (4, 3, -3, 2, -2, 1, -1, 0)
 
+ORDER = (
+    "C0", "X0", "Z02", "Z01", "C1", "Z12", "X1", "Z13", "C2", "X2", "Z21", "Z00", "Z20", "C3",
+    "X3", "C4", "C5", "F0", "Z11", "Z22", "X4", "Z03", "X5", "C6", "Z41", "Z32", "C7", "F1",
+    "X7", "Z33", "Z40", "X6", "F2", "Z42", "Z10", "Z23", "Z31", "F3", "Z61", "Z52", "L0", "Z60",
+    "Z53", "F4", "Z30", "Z62", "F5", "Z43", "Z51", "F7", "L1", "F6", "O", "Z50", "L2", "Z63",
+    "L3", "L4", "G1", "G2", "L5", "L6",
+)
+
 
 def dot(a, b, dims):
     return lax.dot_general(a, b, (dims, ((), ())), preferred_element_type=F32)
 
 
 def kernel(
-    act, cot, projector, first, second, upd, new_first, new_second,
-    act_v, prj_v, cot_v, part_v, other_v, proj_v, term, xr, zz, zx, xz, dir_v, first_v, second_v,
+    act, cot, projector, first, second, dir_v, new_first, new_second,
+    act_v, prj_v, cot_v, part_v, other_v, proj_v, term, xr, zz, zx, xz, first_v, second_v,
     load, cot_load, cot_s, cot_r, part_s, part_r, y_s, y_r, xr_s, xr_r, zz_s, zz_r,
     zx_s, zx_r, xz_s, xz_r, dir_s, dir_r,
 ):
@@ -192,22 +201,19 @@
 
     zz_copies = {}
 
-    def z_step(i):
+    def z_step(i, j):
         s = 1 if STEPS[i] > 0 else -1
-        for j in range(NX):
-            rows = z_rows(i, j)
-            if i == 0:
-                s = 1 if j < 2 else -1
-            elif i in (1, 2):
-                if (j < 2) == (s == 1):
-                    zz_copies[0, j].wait_recv()
-                    term[rows, :] = term[rows, :] + zz[0, j]
-            elif i < 7:
-                zz_copies[i - 2, j].wait_recv()
-                term[rows, :] = term[rows, :] + zz[i - 2, j]
-            zz_copies[i, j] = start(
-                remote(term.at[rows], zz.at[i, j], zz_s.at[i, j], zz_r.at[i, j], at_z(s))
-            )
+        rows = z_rows(i, j)
+        if i == 0:
+            s = 1 if j < 2 else -1
+        elif i in (1, 2):
+            if (j < 2) == (s == 1):
+                zz_copies[0, j].wait_recv()
+                term[rows, :] = term[rows, :] + zz[0, j]
+        else:
+            zz_copies[i - 2, j].wait_recv()
+            term[rows, :] = term[rows, :] + zz[i - 2, j]
+        zz_copies[i, j] = start(remote(term.at[rows], zz.at[i, j], zz_s.at[i, j], zz_r.at[i, j], at_z(s)))
 
     def z_total(j):
         zz_copies[5, j].wait_recv()
@@ -248,8 +254,8 @@
     def adam(lowrank, rows):
         fresh_first = beta_first * first_v[rows, :] + (1.0 - beta_first) * lowrank
         fresh_second = beta_second * second_v[rows, :] + (1.0 - beta_second) * lowrank * lowrank
-        new_first[0, 0, rows, :] = fresh_first
-        new_second[0, 0, rows, :] = fresh_second
+        new_first[rows, :] = fresh_first
+        new_second[rows, :] = fresh_second
         direction = fresh_first / bias_first / (jnp.sqrt(fresh_second / bias_second) + adam_eps)
         dir_v[rows, own_lanes] = direction.astype(BF16)
         n = len(dir_copies)
@@ -259,50 +265,64 @@
             )
         )
 
-    def back_project(n, rows):
-        dir_copies[n].wait_recv()
-        left = dir_v[rows, :]
-        for c in range(8):
-            cols = slice(c * 512, (c + 1) * 512)
-            upd[0, 0, rows, cols] = dot(left, prj_v[cols, :], ((1,), (1,)))
-
-    compute(0), x_open(0), z_step(0)
-    compute(1), x_open(1), z_step(1)
-    compute(2), x_open(2), z_step(2)
-    compute(3), x_open(3), x_forward(0)
-    compute(4), x_open(4), x_forward(1)
-    z_step(3), z_step(4), x_close(0)
-    compute(5), x_open(5), x_forward(2)
-    compute(6), x_open(6), x_close(1)
-    compute(7), x_open(7), x_forward(3)
-    x_close(2), x_forward(4)
-    z_step(5), z_step(6)
-    x_close(3), x_forward(5)
-    x_close(4), x_forward(6)
-    x_close(5), x_forward(7)
-    z_open(), x_close(6)
-    z_forward(1), z_forward(2)
+    run = {
+        "C": compute, "X": x_open, "F": x_forward, "L": x_close, "Z": z_step, "O": z_open, "G": z_forward,
+    }
+    for name in ORDER:
+        run[name[0]](*map(int, name[1:]))
     for c in loads[1 + KCH :]:
         c.wait()
     z_rows_own, x_rows_own = pl.ds(RX, RZ), pl.ds(0, RX)
     adam(z_close(), z_rows_own)
-    back_project(0, z_rows_own)
     adam(x_close(7), x_rows_own)
-    back_project(1, x_rows_own)
+    for c in dir_copies:
+        c.wait_recv()
     for c in sends:
         c.wait_send()
+
+
+def back_project(
+    direction, projector, fresh_first, fresh_second, upd, new_first, new_second,
+    dir_v, prj_v, upd_v, kept_v, load, store, keep,
+):
+    kept = [
+        pltpu.make_async_copy(fresh_first, kept_v.at[0], keep.at[0]),
+        pltpu.make_async_copy(fresh_second, kept_v.at[1], keep.at[1]),
+    ]
+    loads = [pltpu.make_async_copy(direction, dir_v, load.at[0])]
+    parts = [pl.ds(c * COLS, COLS) for c in range(WIDTH // COLS)]
+    for c, part in enumerate(parts):
+        loads.append(pltpu.make_async_copy(projector.at[part], prj_v.at[part], load.at[1 + c]))
+    for c in loads + kept:
+        c.start()
+    loads[0].wait()
+    stores = [
+        pltpu.make_async_copy(kept_v.at[0], new_first.at[0, 0], keep.at[2]),
+        pltpu.make_async_copy(kept_v.at[1], new_second.at[0, 0], keep.at[3]),
+    ]
+    for c, part in enumerate(parts):
+        loads[1 + c].wait()
+        upd_v[:, part] = dot(dir_v[...], prj_v[part, :], ((1,), (1,)))
+        stores.append(pltpu.make_async_copy(upd_v.at[:, part], upd.at[0, 0, :, part], store.at[c]))
+        stores[-1].start()
+    for c in kept:
+        c.wait()
+    for c in stores[:2]:
+        c.start()
+    for c in stores:
+        c.wait()
 
 
 def per_device(activations, cotangents, projector, first_moment, second_moment):
     any_space = pl.BlockSpec(memory_space=pl.ANY)
     vmem = pl.BlockSpec(memory_space=pltpu.VMEM)
     dma = pltpu.SemaphoreType.DMA
-    return pl.pallas_call(
+    direction, fresh_first, fresh_second = pl.pallas_call(
         kernel,
         out_shape=(
-            jax.ShapeDtypeStruct((1, 1, ROWS, WIDTH), F32),
-            jax.ShapeDtypeStruct((1, 1, ROWS, HALF), F32),
-            jax.ShapeDtypeStruct((1, 1, ROWS, HALF), F32),
+            jax.ShapeDtypeStruct((ROWS, RANK), BF16),
+            jax.ShapeDtypeStruct((ROWS, HALF), F32),
+            jax.ShapeDtypeStruct((ROWS, HALF), F32),
         ),
         in_specs=[any_space] * 5,
         out_specs=(vmem, vmem, vmem),
@@ -318,7 +338,6 @@
             pltpu.VMEM((7, NX, RZ, HALF), BF16),
             pltpu.VMEM((7, RX, HALF), BF16),
             pltpu.VMEM((3, RZ, HALF), BF16),
-            pltpu.VMEM((ROWS, RANK), BF16),
             pltpu.VMEM((ROWS, HALF), F32),
             pltpu.VMEM((ROWS, HALF), F32),
             dma((3 + KCH,)),
@@ -345,6 +364,27 @@
         ),
         name="galore_step",
     )(activations, cotangents, projector, first_moment, second_moment)
+    return pl.pallas_call(
+        back_project,
+        out_shape=(
+            jax.ShapeDtypeStruct((1, 1, ROWS, WIDTH), F32),
+            jax.ShapeDtypeStruct((1, 1, ROWS, HALF), F32),
+            jax.ShapeDtypeStruct((1, 1, ROWS, HALF), F32),
+        ),
+        in_specs=[any_space] * 4,
+        out_specs=(any_space,) * 3,
+        scratch_shapes=[
+            pltpu.VMEM((ROWS, RANK), BF16),
+            pltpu.VMEM((WIDTH, RANK), BF16),
+            pltpu.VMEM((ROWS, WIDTH), F32),
+            pltpu.VMEM((2, ROWS, HALF), F32),
+            dma((1 + WIDTH // COLS,)),
+            dma((WIDTH // COLS,)),
+            dma((4,)),
+        ],
+        compiler_params=pltpu.CompilerParams(vmem_limit_bytes=56 * 2**20),
+        name="back_project",
+    )(direction, projector, fresh_first, fresh_second)
 
 
 def solution(mesh):

time: 90.3 us -> 78.2 us (0.87)
  Pallas kernels: 83.7 us -> 76.7 us
  local copies, waits for them, and re-layouts: 5.9 us -> 0 us
    pallas_call x1 -> x2, Pallas kernels: 83.7 us -> 76.7 us  [the longest x1 70.2 us: per_device(): pl.pallas_call(kernel, out_shape=(jax.ShapeDtypeStruct((ROWS, RANK), BF16...]
    unnamed x7 -> x0, local copies, waits for them, and re-layouts: 5.9 us -> none
where the time goes in v2:
time: 78.2 us; the launch traced here: 77.3 us
  Pallas kernels  76.7 us (98%)
    pallas_call x1, Pallas kernels, per_device(): pl.pallas_call(kernel, out_shape=(jax.ShapeDtypeStruct((ROWS, RANK), BF16...  70.2 us
    pallas_call x1, Pallas kernels, per_device(): pl.pallas_call(back_project, out_shape=(jax.ShapeDtypeStruct((1, 1, ROWS,...  6.52 us

profile of v2, /device:TPU:1, one launch (start us, length us, event | category | flops | bytes accessed | tf_op | source)
XLA Modules:
  0.0 77.3 jit_solution(18022599080566752308)
XLA Ops:
  0.6 70.2 %galore_step.1 = (bf16[224,1024]{1,0:T(8,128)(2,1)}, f32[224,512]{1,0:T(8,128)}, f32[224,512]{1,0:T(8,128)}) custom-call(bf16[1,128,4096]{2,1,0:T(8,128)(2,1)} %act.1, bf16[1,256,7168]{2,1,0:T(8,128)(2,1)} %cot.1, bf16[4096,1024]{1,0:T(8,128)(2,1)} %projector.3, f32[1,1,224,512]{3,2,1,0:T(8,128)} %first.1, f32[1,1,224,512]{3,2,1,0:T(8,128)} %second.1), custom_call_target="tpu_custom_call" | custom-call | tf_op jit(solution)/shard_map/galore_step/pallas_call | solution.py:320
  70.8 6.5 %back_project.1 = (f32[1,1,224,4096]{3,2,1,0:T(8,128)}, f32[1,1,224,512]{3,2,1,0:T(8,128)}, f32[1,1,224,512]{3,2,1,0:T(8,128)}) custom-call(bf16[224,1024]{1,0:T(8,128)(2,1)} %get-tuple-element.6.direction, bf16[4096,1024]{1,0:T(8,128)(2,1)} %projector.3, f32[224,512]{1,0:T(8,128)} %get-tuple-element.7.fresh_first, f32[224,512]{1,0:T(8,128)} %get-tuple-element.8.fresh_second), custom_call_target="tpu_custom_call" | custom-call | tf_op jit(solution)/shard_map/back_project/pallas_call | solution.py:367

commit v3 on v0

v3 whole, which is shorter than its diff:
```python
import functools

import jax
import jax.numpy as jnp
from jax import lax
from jax.experimental import pallas as pl
from jax.experimental.pallas import tpu as pltpu
from jax.sharding import PartitionSpec as P

beta_first = 0.9
beta_second = 0.999
bias_first = 1.0 - 0.9**10
bias_second = 1.0 - 0.999**10
adam_eps = 1e-08

NZ, NX, NY = 8, 4, 4
TOK = 128
WIDTH = 4096
RANK = 1024
HALF = 512
ROWS = 224
UNIT = NX * ROWS
HID = NZ * UNIT
RX = 128
RZ = ROWS - RX
LANES = HALF // 2
COLS = 512
F32, BF16 = jnp.float32, jnp.bfloat16
MESH = pl.DeviceIdType.MESH

STEPS = (4, 3, -3, 2, -2, 1, -1, 0)

ORDER = (
    "C00", "X00", "Z004", "Z005", "C10", "Z105", "X10", "C20", "C01", "Z015", "Z204", "X01", "C11", "C31",
    "Z104", "Z205", "X11", "C30", "C40", "X20", "Z014", "C21", "X21", "X30", "Z115", "F02", "X31", "Z215",
    "Z214", "C41", "X42", "Z305", "F12", "C52", "C72", "Z404", "F20", "X72", "Z304", "C62", "Z114", "F21",
    "X62", "Z405", "X52", "Z315", "Z415", "F32", "L02", "Z414", "Z314", "F40", "F41", "Z525", "Z625", "F72",
    "L12", "Z524", "L22", "Z624", "F50", "F51", "F60", "F61", "O72", "L31", "L30", "L40", "L41", "L51",
    "G272", "L60", "G172", "L50", "L61", "L70", "H72", "L71",
)


def dot(a, b, dims):
    return lax.dot_general(a, b, (dims, ((), ())), preferred_element_type=F32)


def kernel(
    act, cot, projector, first, second, dir_v, new_first, new_second,
    act_v, prj_v, cot_v, part_v, other_v, proj_v, tx, tz, xr, zz, zx, xz, first_v, second_v,
    load, cot_load, cot_s, cot_r, part_s, part_r, y_s, y_r, xr_s, xr_r, zz_s, zz_r,
    zx_s, zx_r, xz_s, xz_r, dir_s, dir_r,
):
    dp, core, y = lax.axis_index("dp"), lax.axis_index("fsdp"), lax.axis_index("tensor")
    z, x = dp // NX, dp % NX

    def at_x(k):
        return (z * NX + (x + k + NX) % NX, core, y)

    def at_z(k):
        return (((z + k + NZ) % NZ) * NX + x, core, y)

    def at_y(k):
        return (dp, core, (y + k) % NY)

    sibling = (dp, 1 - core, y)

    def remote(src, dst, send, recv, device):
        return pltpu.make_async_remote_copy(
            src_ref=src, dst_ref=dst, send_sem=send, recv_sem=recv, device_id=device, device_id_type=MESH
        )

    def unit_cols(i):
        return pl.ds(pl.multiple_of(((z + STEPS[i] + NZ) % NZ) * UNIT, UNIT), UNIT)

    own_tok = pl.ds(pl.multiple_of(core * 256, 256), 256)
    get_act = pltpu.make_async_copy(act.at[0], act_v, load.at[0])
    get_act.start()
    get_prj = []
    for r in range(2):
        for h in range(2):
            cols = pl.ds(h * HALF + r * LANES, LANES)
            get_prj.append(pltpu.make_async_copy(projector.at[:, cols], prj_v.at[r, h], load.at[1 + 2 * r + h]))
            get_prj[-1].start()
    get_moments = [
        pltpu.make_async_copy(first.at[0, 0], first_v, load.at[5]),
        pltpu.make_async_copy(second.at[0, 0], second_v, load.at[6]),
    ]
    cot_in = [
        pltpu.make_async_copy(cot.at[0, :, unit_cols(i)], cot_v.at[own_tok, unit_cols(i)], cot_load.at[i])
        for i in range(NZ)
    ]
    cot_x = [
        remote(
            cot_v.at[own_tok, unit_cols(i)], cot_v.at[own_tok, unit_cols(i)], cot_s.at[i], cot_r.at[i], sibling
        )
        for i in range(NZ)
    ]

    barrier = pltpu.get_barrier_semaphore()
    for device in (sibling, at_y(1), at_y(2), at_y(3), at_x(1), at_x(-1), at_z(1), at_z(-1)):
        pl.semaphore_signal(barrier, inc=1, device_id=device, device_id_type=MESH)
    pl.semaphore_wait(barrier, 8)

    swap = [
        remote(part_v.at[r, 1 - core], other_v.at[r], part_s.at[r], part_r.at[r], sibling) for r in range(2)
    ]
    own_rows = pl.ds(pl.multiple_of(y * TOK, TOK), TOK)
    gather = [
        [
            remote(proj_v.at[r, own_rows], proj_v.at[r, own_rows], y_s.at[r, k - 1], y_r.at[r, k - 1], at_y(k))
            for k in (2, 1, 3)
        ]
        for r in range(2)
    ]
    get_act.wait()
    for r in range(2):
        for h in range(2):
            get_prj[2 * r + h].wait()
        if r == 1:
            for c in cot_in + get_moments:
                c.start()
        part_v[r, 1 - core] = dot(act_v[...], prj_v[r, 1 - core], ((1,), (0,)))
        swap[r].start()
        part_v[r, core] = dot(act_v[...], prj_v[r, core], ((1,), (0,)))
        swap[r].wait_recv()
        proj_v[r, own_rows, :] = (part_v[r, core] + other_v[r]).astype(BF16)
        for c in gather[r]:
            c.start()
    for i in range(NZ):
        cot_in[i].wait()
        cot_x[i].start()

    sends = cot_x + swap + gather[0] + gather[1]
    pending = {}

    def send(key, src, dst, send_sem, recv_sem, device):
        copy = remote(src, dst, send_sem, recv_sem, device)
        copy.start()
        sends.append(copy)
        pending[key] = copy

    def parts(r):
        return (0, 1) if r == 2 else (r,)

    def pick(r):
        return slice(None) if r == 2 else r

    def need(kind, r):
        for half in parts(r) + (2,):
            copy = pending.pop(kind + (half,), None)
            if copy is not None:
                copy.wait_recv()

    gathered, exchanged = set(), set()

    def compute(i, r):
        if i not in exchanged:
            exchanged.add(i)
            cot_x[i].wait_recv()
        for half in parts(r):
            if half not in gathered:
                gathered.add(half)
                for c in gather[half]:
                    c.wait_recv()
            block = dot(cot_v[:, unit_cols(i)], proj_v[half], ((0,), (0,))).astype(BF16)
            for column in range(NX):
                j, first_row = (column - x + NX) % NX, column * ROWS
                tx[half, i, j] = block[first_row : first_row + RX]
                tz[half, i, j] = block[first_row + RX : first_row + ROWS]

    def x_send(i, r, n, j, k):
        h = r % 2
        send(
            ("x", i, n, r), tx.at[pick(r), i, j % NX], xr.at[pick(r), i, n],
            xr_s.at[h, i, n], xr_r.at[h, i, n], at_x(k),
        )

    def x_open(i, r):
        s = 1 - 2 * (i % 2)
        x_send(i, r, 0, 2, s)
        x_send(i, r, 2, -s, -s)

    def x_forward(i, r):
        s = 1 - 2 * (i % 2)
        need(("x", i, 0), r)
        for half in parts(r):
            tx[half, i, s % NX] = tx[half, i, s % NX] + xr[half, i, 0]
        x_send(i, r, 1, s, s)

    def x_close(i, r):
        s = 1 if STEPS[i] > 0 else -1
        need(("x", i, 1), r)
        need(("x", i, 2), r)
        earlier = {0: (), 1: (0,), 2: (0,), 7: (5, 6)}.get(i, (i - 2,))
        for e in earlier:
            need(("zx", e), r if e else (0 if s == 1 else 1))
        for half in parts(r):
            total = tx[half, i, 0].astype(F32) + xr[half, i, 1].astype(F32) + xr[half, i, 2].astype(F32)
            for e in earlier:
                if e or (half == 0) == (s == 1):
                    total = total + zx[half, e].astype(F32)
            if i == 7:
                adam(total, pl.ds(0, RX), half, 0)
            else:
                tx[half, i, 0] = total.astype(BF16)
        if i == 0:
            for h, k in enumerate((1, -1)):
                send(("zx", 0, h), tx.at[h, 0, 0], zx.at[h, 0], zx_s.at[h, 0], zx_r.at[h, 0], at_z(k))
        elif i < 7:
            h = r % 2
            send(("zx", i, r), tx.at[pick(r), i, 0], zx.at[pick(r), i], zx_s.at[h, i], zx_r.at[h, i], at_z(s))

    def z_step(i, r, g):
        first, count = ((g - 4) * 2, 2) if g > 3 else (g, 1)
        s = 1 if STEPS[i] > 0 else -1
        if i == 0:
            s = 1 if first < 2 else -1
        elif i > 2 or (first < 2) == (s == 1):
            e = max(i - 2, 0)
            for j in range(first, first + count):
                need_z(e, j, r)
                for half in parts(r):
                    tz[half, i, j] = tz[half, i, j] + zz[half, e, j]
        h, blocks = r % 2, pl.ds(first, count)
        send(
            ("z", i, g, r), tz.at[pick(r), i, blocks], zz.at[pick(r), i, blocks],
            zz_s.at[h, i, first], zz_r.at[h, i, first], at_z(s),
        )

    def need_z(e, j, r):
        need(("z", e, j), r)
        need(("z", e, 4 + j // 2), r)

    def z_total(j, half):
        for e in (5, 6):
            need_z(e, j, 2)
        return tz[half, 7, j].astype(F32) + zz[half, 5, j].astype(F32) + zz[half, 6, j].astype(F32)

    def z_open(i, r):
        for h, k in enumerate((1, -1)):
            tz[h, 7, 2] = z_total(2, h).astype(BF16)
            send(("xz", 0, h), tz.at[h, 7, 2], xz.at[h, 0], xz_s.at[h, 0], xz_r.at[h, 0], at_x(k))

    def z_forward(n, i, r):
        s = 1 if n == 1 else -1
        j = s % NX
        need(("xz", 0), 0 if s == 1 else 1)
        for half in range(2):
            total = z_total(j, half)
            if (half == 0) == (s == 1):
                total = total + xz[half, 0].astype(F32)
            tz[half, 7, j] = total.astype(BF16)
        send(("xz", n, 2), tz.at[:, 7, j], xz.at[:, n], xz_s.at[0, n], xz_r.at[0, n], at_x(s))

    def z_close(i, r):
        for n in (1, 2):
            need(("xz", n), 2)
        for half in range(2):
            total = z_total(0, half)
            adam(total + xz[half, 1].astype(F32) + xz[half, 2].astype(F32), pl.ds(RX, RZ), half, 1)


    def adam(lowrank, rows, r, n):
        lanes = pl.ds(r * LANES, LANES)
        for c in get_moments:
            c.wait()
        get_moments.clear()
        fresh_first = beta_first * first_v[rows, lanes] + (1.0 - beta_first) * lowrank
        fresh_second = beta_second * second_v[rows, lanes] + (1.0 - beta_second) * lowrank * lowrank
        new_first[rows, lanes] = fresh_first
        new_second[rows, lanes] = fresh_second
        direction = fresh_first / bias_first / (jnp.sqrt(fresh_second / bias_second) + adam_eps)
        own = pl.ds(pl.multiple_of(core * HALF + r * LANES, LANES), LANES)
        dir_v[rows, own] = direction.astype(BF16)
        send(
            ("dir", n, r), dir_v.at[rows, own], dir_v.at[rows, own], dir_s.at[r, n], dir_r.at[r, n], sibling
        )

    run = {
        "C": compute, "X": x_open, "F": x_forward, "L": x_close,
        "Z": z_step, "O": z_open, "G": z_forward, "H": z_close,
    }
    for name in ORDER:
        run[name[0]](*map(int, name[1:]))
    for n in range(2):
        need(("dir", n), 2)
    assert not pending
    for c in sends:
        c.wait_send()


def back_project(
    direction, projector, fresh_first, fresh_second, upd, new_first, new_second,
    dir_v, prj_v, upd_v, kept_v, load, store, keep,
):
    kept = [
        pltpu.make_async_copy(fresh_first, kept_v.at[0], keep.at[0]),
        pltpu.make_async_copy(fresh_second, kept_v.at[1], keep.at[1]),
    ]
    loads = [pltpu.make_async_copy(direction, dir_v, load.at[0])]
    parts = [pl.ds(c * COLS, COLS) for c in range(WIDTH // COLS)]
    for c, part in enumerate(parts):
        loads.append(pltpu.make_async_copy(projector.at[part], prj_v.at[part], load.at[1 + c]))
    for c in loads + kept:
        c.start()
    loads[0].wait()
    stores = [
        pltpu.make_async_copy(kept_v.at[0], new_first.at[0, 0], keep.at[2]),
        pltpu.make_async_copy(kept_v.at[1], new_second.at[0, 0], keep.at[3]),
    ]
    for c, part in enumerate(parts):
        loads[1 + c].wait()
        upd_v[:, part] = dot(dir_v[...], prj_v[part, :], ((1,), (1,)))
        stores.append(pltpu.make_async_copy(upd_v.at[:, part], upd.at[0, 0, :, part], store.at[c]))
        stores[-1].start()
    for c in kept:
        c.wait()
    for c in stores[:2]:
        c.start()
    for c in stores:
        c.wait()


def per_device(activations, cotangents, projector, first_moment, second_moment):
    any_space = pl.BlockSpec(memory_space=pl.ANY)
    vmem = pl.BlockSpec(memory_space=pltpu.VMEM)
    dma = pltpu.SemaphoreType.DMA
    direction, fresh_first, fresh_second = pl.pallas_call(
        kernel,
        out_shape=(
            jax.ShapeDtypeStruct((ROWS, RANK), BF16),
            jax.ShapeDtypeStruct((ROWS, HALF), F32),
            jax.ShapeDtypeStruct((ROWS, HALF), F32),
        ),
        in_specs=[any_space] * 5,
        out_specs=(vmem, vmem, vmem),
        scratch_shapes=[
            pltpu.VMEM((TOK, WIDTH), BF16),
            pltpu.VMEM((2, 2, WIDTH, LANES), BF16),
            pltpu.VMEM((512, HID), BF16),
            pltpu.VMEM((2, 2, TOK, LANES), F32),
            pltpu.VMEM((2, TOK, LANES), F32),
            pltpu.VMEM((2, 512, LANES), BF16),
            pltpu.VMEM((2, 8, NX, RX, LANES), BF16),
            pltpu.VMEM((2, 8, NX, RZ, LANES), BF16),
            pltpu.VMEM((2, 8, 3, RX, LANES), BF16),
            pltpu.VMEM((2, 7, NX, RZ, LANES), BF16),
            pltpu.VMEM((2, 7, RX, LANES), BF16),
            pltpu.VMEM((2, 3, RZ, LANES), BF16),
            pltpu.VMEM((ROWS, HALF), F32),
            pltpu.VMEM((ROWS, HALF), F32),
            dma((7,)),
            dma((8,)),
            dma((8,)),
            dma((8,)),
            dma((2,)),
            dma((2,)),
            dma((2, 3)),
            dma((2, 3)),
            dma((2, 8, 3)),
            dma((2, 8, 3)),
            dma((2, 7, NX)),
            dma((2, 7, NX)),
            dma((2, 8)),
            dma((2, 8)),
            dma((2, 4)),
            dma((2, 4)),
            dma((2, 2)),
            dma((2, 2)),
        ],
        compiler_params=pltpu.CompilerParams(
            collective_id=0, has_side_effects=True, vmem_limit_bytes=56 * 2**20
        ),
        name="galore_step",
    )(activations, cotangents, projector, first_moment, second_moment)
    return pl.pallas_call(
        back_project,
        out_shape=(
            jax.ShapeDtypeStruct((1, 1, ROWS, WIDTH), F32),
            jax.ShapeDtypeStruct((1, 1, ROWS, HALF), F32),
            jax.ShapeDtypeStruct((1, 1, ROWS, HALF), F32),
        ),
        in_specs=[any_space] * 4,
        out_specs=(any_space,) * 3,
        scratch_shapes=[
            pltpu.VMEM((ROWS, RANK), BF16),
            pltpu.VMEM((WIDTH, RANK), BF16),
            pltpu.VMEM((ROWS, WIDTH), F32),
            pltpu.VMEM((2, ROWS, HALF), F32),
            dma((1 + WIDTH // COLS,)),
            dma((WIDTH // COLS,)),
            dma((4,)),
        ],
        compiler_params=pltpu.CompilerParams(vmem_limit_bytes=56 * 2**20),
        name="back_project",
    )(direction, projector, fresh_first, fresh_second)


def solution(mesh):
    return jax.shard_map(
        per_device,
        mesh=mesh,
        in_specs=(
            P(None, ("dp", "tensor"), "fsdp"),
            P(None, ("dp", "fsdp"), "tensor"),
            P("fsdp", None),
            P(None, "tensor", "dp", "fsdp"),
            P(None, "tensor", "dp", "fsdp"),
        ),
        out_specs=(
            P(None, "tensor", "dp", "fsdp"),
            P(None, "tensor", "dp", "fsdp"),
            P(None, "tensor", "dp", "fsdp"),
        ),
        check_vma=False,
    )
```

time: 307 us -> 74.1 us (0.24)
  waiting for transfers between devices: 229 us -> 0 us
  Pallas kernels: 0 us -> 73.4 us
  blocking collectives: 24.7 us -> 0 us
  matrix products: 21.7 us -> 0 us
  local copies, waits for them, and re-layouts: 16 us -> 0 us
  between operations: 14.1 us -> 0.64 us
    unnamed x3 -> x0, waiting for transfers between devices: 222 us -> none
    pallas_call x0 -> x2, Pallas kernels: none -> 73.4 us  [the longest x1 66.9 us: per_device(): pl.pallas_call(kernel, out_shape=(jax.ShapeDtypeStruct((ROWS, RANK), BF16...]
    dot_general x3 -> x0, matrix products: 21.7 us -> none  [the longest x1 9.14 us: per_device(): lax.dot_general(gathered, projected, (((0,), (0,)), ((), ())), preferred_...]
    all_gather x2 -> x0, blocking collectives: 16.7 us -> none  [the longest x1 10.3 us: per_device(): projected = lax.all_gather(own_share, 'tensor', axis=0, tiled=True)]
    unnamed x12 -> x0, local copies, waits for them, and re-layouts: 15.9 us -> none
    psum x1 -> x0, blocking collectives: 7.93 us -> none  [per_device(): summed = lax.psum(partial_proj, 'fsdp')]
    all_gather x1 -> x0, waiting for transfers between devices: 6.69 us -> none  [per_device(): gathered = lax.all_gather(cotangents[0], 'fsdp', axis=0, tiled=True)]
  transfers between devices with their start and end apart: 2 -> 0, of which waited for: 2 -> 0; matrix products, arithmetic and copies ran while one was open for 2% -> 0% of each run, Pallas kernels for 0% -> 0%
where the time goes in v3:
time: 74.1 us; the launch traced here: 74 us
  Pallas kernels  73.4 us (99%)
    pallas_call x1, Pallas kernels, per_device(): pl.pallas_call(kernel, out_shape=(jax.ShapeDtypeStruct((ROWS, RANK), BF16...  66.9 us
    pallas_call x1, Pallas kernels, per_device(): pl.pallas_call(back_project, out_shape=(jax.ShapeDtypeStruct((1, 1, ROWS,...  6.52 us

profile of v3, /device:TPU:1, one launch (start us, length us, event | category | flops | bytes accessed | tf_op | source)
XLA Modules:
  0.0 74.0 jit_solution(15762951075408674814)
XLA Ops:
  0.6 66.9 %galore_step.1 = (bf16[224,1024]{1,0:T(8,128)(2,1)}, f32[224,512]{1,0:T(8,128)}, f32[224,512]{1,0:T(8,128)}) custom-call(bf16[1,128,4096]{2,1,0:T(8,128)(2,1)} %act.1, bf16[1,256,7168]{2,1,0:T(8,128)(2,1)} %cot.1, bf16[4096,1024]{1,0:T(8,128)(2,1)} %projector.3, f32[1,1,224,512]{3,2,1,0:T(8,128)} %first.1, f32[1,1,224,512]{3,2,1,0:T(8,128)} %second.1), custom_call_target="tpu_custom_call" | custom-call | tf_op jit(solution)/shard_map/galore_step/pallas_call | solution.py:328
  67.5 6.5 %back_project.1 = (f32[1,1,224,4096]{3,2,1,0:T(8,128)}, f32[1,1,224,512]{3,2,1,0:T(8,128)}, f32[1,1,224,512]{3,2,1,0:T(8,128)}) custom-call(bf16[224,1024]{1,0:T(8,128)(2,1)} %get-tuple-element.6.direction, bf16[4096,1024]{1,0:T(8,128)(2,1)} %projector.3, f32[224,512]{1,0:T(8,128)} %get-tuple-element.7.fresh_first, f32[224,512]{1,0:T(8,128)} %get-tuple-element.8.fresh_second), custom_call_target="tpu_custom_call" | custom-call | tf_op jit(solution)/shard_map/back_project/pallas_call | solution.py:376

commit v4 on v3

--- a/solution.py
+++ b/solution.py
@@ -80,7 +80,8 @@
         for h in range(2):
             cols = pl.ds(h * HALF + r * LANES, LANES)
             get_prj.append(pltpu.make_async_copy(projector.at[:, cols], prj_v.at[r, h], load.at[1 + 2 * r + h]))
-            get_prj[-1].start()
+            if r == 0:
+                get_prj[-1].start()
     get_moments = [
         pltpu.make_async_copy(first.at[0, 0], first_v, load.at[5]),
         pltpu.make_async_copy(second.at[0, 0], second_v, load.at[6]),
@@ -116,9 +117,8 @@
     for r in range(2):
         for h in range(2):
             get_prj[2 * r + h].wait()
-        if r == 1:
-            for c in cot_in + get_moments:
-                c.start()
+        for c in (get_prj[2:] if r == 0 else cot_in + get_moments):
+            c.start()
         part_v[r, 1 - core] = dot(act_v[...], prj_v[r, 1 - core], ((1,), (0,)))
         swap[r].start()
         part_v[r, core] = dot(act_v[...], prj_v[r, core], ((1,), (0,)))
@@ -289,34 +289,18 @@
         c.wait_send()
 
 
-def back_project(
-    direction, projector, fresh_first, fresh_second, upd, new_first, new_second,
-    dir_v, prj_v, upd_v, kept_v, load, store, keep,
-):
-    kept = [
-        pltpu.make_async_copy(fresh_first, kept_v.at[0], keep.at[0]),
-        pltpu.make_async_copy(fresh_second, kept_v.at[1], keep.at[1]),
-    ]
-    loads = [pltpu.make_async_copy(direction, dir_v, load.at[0])]
-    parts = [pl.ds(c * COLS, COLS) for c in range(WIDTH // COLS)]
-    for c, part in enumerate(parts):
-        loads.append(pltpu.make_async_copy(projector.at[part], prj_v.at[part], load.at[1 + c]))
-    for c in loads + kept:
+def back_project(direction, projector, fresh_first, fresh_second, upd, new_first, new_second, upd_v, store):
+    stores = [
+        pltpu.make_async_copy(fresh_first, new_first.at[0, 0], store.at[0]),
+        pltpu.make_async_copy(fresh_second, new_second.at[0, 0], store.at[1]),
+    ]
+    for c in stores:
         c.start()
-    loads[0].wait()
-    stores = [
-        pltpu.make_async_copy(kept_v.at[0], new_first.at[0, 0], keep.at[2]),
-        pltpu.make_async_copy(kept_v.at[1], new_second.at[0, 0], keep.at[3]),
-    ]
-    for c, part in enumerate(parts):
-        loads[1 + c].wait()
-        upd_v[:, part] = dot(dir_v[...], prj_v[part, :], ((1,), (1,)))
-        stores.append(pltpu.make_async_copy(upd_v.at[:, part], upd.at[0, 0, :, part], store.at[c]))
+    for c in range(WIDTH // COLS):
+        part = pl.ds(c * COLS, COLS)
+        upd_v[:, part] = dot(direction[...], projector[part, :], ((1,), (1,)))
+        stores.append(pltpu.make_async_copy(upd_v.at[:, part], upd.at[0, 0, :, part], store.at[2 + c]))
         stores[-1].start()
-    for c in kept:
-        c.wait()
-    for c in stores[:2]:
-        c.start()
     for c in stores:
         c.wait()
 
@@ -369,7 +353,7 @@
             dma((2, 2)),
         ],
         compiler_params=pltpu.CompilerParams(
-            collective_id=0, has_side_effects=True, vmem_limit_bytes=56 * 2**20
+            collective_id=0, has_side_effects=True, vmem_limit_bytes=105 * 2**19
         ),
         name="galore_step",
     )(activations, cotangents, projector, first_moment, second_moment)
@@ -380,18 +364,10 @@
             jax.ShapeDtypeStruct((1, 1, ROWS, HALF), F32),
             jax.ShapeDtypeStruct((1, 1, ROWS, HALF), F32),
         ),
-        in_specs=[any_space] * 4,
+        in_specs=[vmem] * 4,
         out_specs=(any_space,) * 3,
-        scratch_shapes=[
-            pltpu.VMEM((ROWS, RANK), BF16),
-            pltpu.VMEM((WIDTH, RANK), BF16),
-            pltpu.VMEM((ROWS, WIDTH), F32),
-            pltpu.VMEM((2, ROWS, HALF), F32),
-            dma((1 + WIDTH // COLS,)),
-            dma((WIDTH // COLS,)),
-            dma((4,)),
-        ],
-        compiler_params=pltpu.CompilerParams(vmem_limit_bytes=56 * 2**20),
+        scratch_shapes=[pltpu.VMEM((ROWS, WIDTH), F32), dma((2 + WIDTH // COLS,))],
+        compiler_params=pltpu.CompilerParams(vmem_limit_bytes=12 * 2**20),
         name="back_project",
     )(direction, projector, fresh_first, fresh_second)
 

time: 74.1 us -> 70.1 us (0.946)
  Pallas kernels: 73.4 us -> 69.3 us
    pallas_call x1, Pallas kernels: 6.52 us -> 3.46 us  [per_device(): pl.pallas_call(back_project, out_shape=(jax.ShapeDtypeStruct((1, 1, ROWS,...]
    pallas_call x1, Pallas kernels: 66.9 us -> 65.9 us  [per_device(): pl.pallas_call(kernel, out_shape=(jax.ShapeDtypeStruct((ROWS, RANK), BF16...]
where the time goes in v4:
time: 70.1 us; the launch traced here: 70 us
  Pallas kernels  69.3 us (99%)
    pallas_call x1, Pallas kernels, per_device(): pl.pallas_call(kernel, out_shape=(jax.ShapeDtypeStruct((ROWS, RANK), BF16...  65.9 us
    pallas_call x1, Pallas kernels, per_device(): pl.pallas_call(back_project, out_shape=(jax.ShapeDtypeStruct((1, 1, ROWS,...  3.46 us

profile of v4, /device:TPU:1, one launch (start us, length us, event | category | flops | bytes accessed | tf_op | source)
XLA Modules:
  0.0 70.0 jit_solution(16309352820424911224)
XLA Ops:
  0.6 0.0 copy-start
  0.6 65.9 %galore_step.1 = (bf16[224,1024]{1,0:T(8,128)(2,1)S(1)}, f32[224,512]{1,0:T(8,128)S(1)}, f32[224,512]{1,0:T(8,128)S(1)}) custom-call(bf16[1,128,4096]{2,1,0:T(8,128)(2,1)} %act.1, bf16[1,256,7168]{2,1,0:T(8,128)(2,1)} %cot.1, bf16[4096,1024]{1,0:T(8,128)(2,1)} %projector.3, f32[1,1,224,512]{3,2,1,0:T(8,128)} %first.1, f32[1,1,224,512]{3,2,1,0:T(8,128)} %second.1), custom_call_target="tpu_custom_call" | custom-call | tf_op jit(solution)/shard_map/galore_step/pallas_call | solution.py:312
  66.5 0.0 copy-done
  66.5 3.5 %back_project.1 = (f32[1,1,224,4096]{3,2,1,0:T(8,128)}, f32[1,1,224,512]{3,2,1,0:T(8,128)}, f32[1,1,224,512]{3,2,1,0:T(8,128)}) custom-call(bf16[224,1024]{1,0:T(8,128)(2,1)S(1)} %get-tuple-element.6.direction, bf16[4096,1024]{1,0:T(8,128)(2,1)S(1)} %copy-done, f32[224,512]{1,0:T(8,128)S(1)} %get-tuple-element.7.fresh_first, ...), custom_call_target="tpu_custom_call" | custom-call | tf_op jit(solution)/shard_map/back_project/pallas_call | solution.py:360
Async XLA Ops:
  0.6 65.9 %copy-start = (bf16[4096,1024]{1,0:T(8,128)(2,1)S(1)}, bf16[4096,1024]{1,0:T(8,128)(2,1)}, u32[]{:S(2)}) copy-start(bf16[4096,1024]{1,0:T(8,128)(2,1)} %projector.3) | copy-start | bytes 25165828

commit v5 on v4

--- a/solution.py
+++ b/solution.py
@@ -31,12 +31,12 @@
 STEPS = (4, 3, -3, 2, -2, 1, -1, 0)
 
 ORDER = (
-    "C00", "X00", "Z004", "Z005", "C10", "Z105", "X10", "C20", "C01", "Z015", "Z204", "X01", "C11", "C31",
-    "Z104", "Z205", "X11", "C30", "C40", "X20", "Z014", "C21", "X21", "X30", "Z115", "F02", "X31", "Z215",
-    "Z214", "C41", "X42", "Z305", "F12", "C52", "C72", "Z404", "F20", "X72", "Z304", "C62", "Z114", "F21",
-    "X62", "Z405", "X52", "Z315", "Z415", "F32", "L02", "Z414", "Z314", "F40", "F41", "Z525", "Z625", "F72",
-    "L12", "Z524", "L22", "Z624", "F50", "F51", "F60", "F61", "O72", "L31", "L30", "L40", "L41", "L51",
-    "G272", "L60", "G172", "L50", "L61", "L70", "H72", "L71",
+    "C00", "Z004", "X00", "Z005", "C10", "X10", "Z105", "C20", "C01", "Z015", "X01", "X20", "Z204", "C30",
+    "Z014", "C11", "Z115", "X11", "C41", "C40", "Z205", "C21", "X21", "Z104", "F02", "X30", "C31", "Z215",
+    "X31", "C62", "Z114", "Z305", "X42", "C72", "Z404", "F12", "X62", "C52", "Z315", "F22", "Z214", "Z405",
+    "X72", "X52", "Z304", "Z415", "L02", "F32", "Z314", "Z414", "Z523", "Z522", "F40", "F41", "Z623", "Z622",
+    "F60", "F61", "L12", "Z521", "Z520", "L22", "F70", "Z621", "Z620", "F71", "F50", "F51", "O72", "L30",
+    "L31", "L40", "L41", "L50", "G172", "G272", "L60", "L51", "L61", "L70", "H72", "L71",
 )
 
 
@@ -68,6 +68,10 @@
         return pltpu.make_async_remote_copy(
             src_ref=src, dst_ref=dst, send_sem=send, recv_sem=recv, device_id=device, device_id_type=MESH
         )
+
+    barrier = pltpu.get_barrier_semaphore()
+    for device in (sibling, at_y(1), at_y(2), at_y(3), at_x(1), at_x(-1), at_z(1), at_z(-1)):
+        pl.semaphore_signal(barrier, inc=1, device_id=device, device_id_type=MESH)
 
     def unit_cols(i):
         return pl.ds(pl.multiple_of(((z + STEPS[i] + NZ) % NZ) * UNIT, UNIT), UNIT)
@@ -97,9 +101,6 @@
         for i in range(NZ)
     ]
 
-    barrier = pltpu.get_barrier_semaphore()
-    for device in (sibling, at_y(1), at_y(2), at_y(3), at_x(1), at_x(-1), at_z(1), at_z(-1)):
-        pl.semaphore_signal(barrier, inc=1, device_id=device, device_id_type=MESH)
     pl.semaphore_wait(barrier, 8)
 
     swap = [

time: 70.1 us -> 70 us (level)
  no operation moved by 1% of the time
where the time goes in v5:
time: 70 us; the launch traced here: 69.9 us
  Pallas kernels  69.2 us (99%)
    pallas_call x1, Pallas kernels, per_device(): pl.pallas_call(kernel, out_shape=(jax.ShapeDtypeStruct((ROWS, RANK), BF16...  65.8 us
    pallas_call x1, Pallas kernels, per_device(): pl.pallas_call(back_project, out_shape=(jax.ShapeDtypeStruct((1, 1, ROWS,...  3.44 us

profile of v5, /device:TPU:1, one launch (start us, length us, event | category | flops | bytes accessed | tf_op | source)
XLA Modules:
  0.0 69.9 jit_solution(1682777083775813871)
XLA Ops:
  0.6 0.0 copy-start
  0.6 65.8 %galore_step.1 = (bf16[224,1024]{1,0:T(8,128)(2,1)S(1)}, f32[224,512]{1,0:T(8,128)S(1)}, f32[224,512]{1,0:T(8,128)S(1)}) custom-call(bf16[1,128,4096]{2,1,0:T(8,128)(2,1)} %act.1, bf16[1,256,7168]{2,1,0:T(8,128)(2,1)} %cot.1, bf16[4096,1024]{1,0:T(8,128)(2,1)} %projector.3, f32[1,1,224,512]{3,2,1,0:T(8,128)} %first.1, f32[1,1,224,512]{3,2,1,0:T(8,128)} %second.1), custom_call_target="tpu_custom_call" | custom-call | tf_op jit(solution)/shard_map/galore_step/pallas_call | solution.py:313
  66.4 0.0 copy-done
  66.4 3.4 %back_project.1 = (f32[1,1,224,4096]{3,2,1,0:T(8,128)}, f32[1,1,224,512]{3,2,1,0:T(8,128)}, f32[1,1,224,512]{3,2,1,0:T(8,128)}) custom-call(bf16[224,1024]{1,0:T(8,128)(2,1)S(1)} %get-tuple-element.6.direction, bf16[4096,1024]{1,0:T(8,128)(2,1)S(1)} %copy-done, f32[224,512]{1,0:T(8,128)S(1)} %get-tuple-element.7.fresh_first, ...), custom_call_target="tpu_custom_call" | custom-call | tf_op jit(solution)/shard_map/back_project/pallas_call | solution.py:361
Async XLA Ops:
  0.6 65.8 %copy-start = (bf16[4096,1024]{1,0:T(8,128)(2,1)S(1)}, bf16[4096,1024]{1,0:T(8,128)(2,1)}, u32[]{:S(2)}) copy-start(bf16[4096,1024]{1,0:T(8,128)(2,1)} %projector.3) | copy-start | bytes 25165828

commit v6 on v5

--- a/solution.py
+++ b/solution.py
@@ -82,7 +82,8 @@
     get_prj = []
     for r in range(2):
         for h in range(2):
-            cols = pl.ds(h * HALF + r * LANES, LANES)
+            share = core if h else 1 - core
+            cols = pl.ds(pl.multiple_of(share * HALF + r * LANES, LANES), LANES)
             get_prj.append(pltpu.make_async_copy(projector.at[:, cols], prj_v.at[r, h], load.at[1 + 2 * r + h]))
             if r == 0:
                 get_prj[-1].start()
@@ -116,13 +117,13 @@
     ]
     get_act.wait()
     for r in range(2):
-        for h in range(2):
-            get_prj[2 * r + h].wait()
+        get_prj[2 * r].wait()
+        part_v[r, 1 - core] = dot(act_v[...], prj_v[r, 0], ((1,), (0,)))
+        swap[r].start()
+        get_prj[2 * r + 1].wait()
         for c in (get_prj[2:] if r == 0 else cot_in + get_moments):
             c.start()
-        part_v[r, 1 - core] = dot(act_v[...], prj_v[r, 1 - core], ((1,), (0,)))
-        swap[r].start()
-        part_v[r, core] = dot(act_v[...], prj_v[r, core], ((1,), (0,)))
+        part_v[r, core] = dot(act_v[...], prj_v[r, 1], ((1,), (0,)))
         swap[r].wait_recv()
         proj_v[r, own_rows, :] = (part_v[r, core] + other_v[r]).astype(BF16)
         for c in gather[r]:

time: 70 us -> 69.3 us (0.990)
  no operation moved by 1% of the time
where the time goes in v6:
time: 69.3 us; the launch traced here: 69.2 us
  Pallas kernels  68.6 us (99%)
    pallas_call x1, Pallas kernels, per_device(): pl.pallas_call(kernel, out_shape=(jax.ShapeDtypeStruct((ROWS, RANK), BF16...  65.1 us
    pallas_call x1, Pallas kernels, per_device(): pl.pallas_call(back_project, out_shape=(jax.ShapeDtypeStruct((1, 1, ROWS,...  3.44 us

profile of v6, /device:TPU:1, one launch (start us, length us, event | category | flops | bytes accessed | tf_op | source)
XLA Modules:
  0.0 69.2 jit_solution(17153638338145832588)
XLA Ops:
  0.6 0.0 copy-start
  0.6 65.1 %galore_step.1 = (bf16[224,1024]{1,0:T(8,128)(2,1)S(1)}, f32[224,512]{1,0:T(8,128)S(1)}, f32[224,512]{1,0:T(8,128)S(1)}) custom-call(bf16[1,128,4096]{2,1,0:T(8,128)(2,1)} %act.1, bf16[1,256,7168]{2,1,0:T(8,128)(2,1)} %cot.1, bf16[4096,1024]{1,0:T(8,128)(2,1)} %projector.3, f32[1,1,224,512]{3,2,1,0:T(8,128)} %first.1, f32[1,1,224,512]{3,2,1,0:T(8,128)} %second.1), custom_call_target="tpu_custom_call" | custom-call | tf_op jit(solution)/shard_map/galore_step/pallas_call | solution.py:314
  65.8 0.0 copy-done
  65.8 3.4 %back_project.1 = (f32[1,1,224,4096]{3,2,1,0:T(8,128)}, f32[1,1,224,512]{3,2,1,0:T(8,128)}, f32[1,1,224,512]{3,2,1,0:T(8,128)}) custom-call(bf16[224,1024]{1,0:T(8,128)(2,1)S(1)} %get-tuple-element.6.direction, bf16[4096,1024]{1,0:T(8,128)(2,1)S(1)} %copy-done, f32[224,512]{1,0:T(8,128)S(1)} %get-tuple-element.7.fresh_first, ...), custom_call_target="tpu_custom_call" | custom-call | tf_op jit(solution)/shard_map/back_project/pallas_call | solution.py:362
Async XLA Ops:
  0.6 65.2 %copy-start = (bf16[4096,1024]{1,0:T(8,128)(2,1)S(1)}, bf16[4096,1024]{1,0:T(8,128)(2,1)}, u32[]{:S(2)}) copy-start(bf16[4096,1024]{1,0:T(8,128)(2,1)} %projector.3) | copy-start | bytes 25165828
